TPU v7x, 32 devices: a whole 2x2x4 slice. The times are simulated.
32 devices in a mesh: ha: 4 (over y, x), wa: 4 (over z), ta: 2 (over core).
Axes of the slice: x: 2, y: 2, z: 4, core: 2. Of those that a mesh axis runs over, the one named last changes fastest.
Arguments:
- hidden_states: bfloat16 [2, 96, 32, 5120], P(None, 'ha', 'wa', 'ta'), may hold values from -60 to 60
- queries: bfloat16 [2, 96, 32, 5120], P(None, 'ha', 'wa', 'ta'), may hold values from -120 to 120
- keys_values: bfloat16 [2, 2, 96, 32, 5120], P(None, None, 'ha', 'wa', 'ta'), may hold values from -16 to 16
- out_weight: bfloat16 [5120, 5120], P('ta', 'wa'), may hold values from -0.078125 to 0.078125
- mod_table: float32 [50, 3, 5120], P(None, None, 'ta'), may hold values from -4 to 4
- windows: int32 [40, 2], P('ta'), may hold values from 0 to 1, as said below
- step_index: int32 [1], replicated, may hold values from 0 to 49
Outputs:
- residual_out: bfloat16 [2, 96, 32, 5120], P(None, 'ha', 'wa', 'ta')
- ffn_input: bfloat16 [2, 96, 32, 5120], P(None, 'ha', 'wa', 'ta')
Inputs may be any that keep to these rules, and one draw needn't show every extreme that they name: `windows`: some head has both radii equal to 1.
All inputs are finite; a program needn't handle non-finite values.
Results may differ from a plain program's by a relative error of at most 0.0085.
Values may be sent and summed in bfloat16 or wider, within the bound.
No kernel may reach another device: no remote copies, remote signals or barrier semaphores. Data moves between devices by JAX's collectives and lax.ppermute only.
A program may use at most 128 MiB of HBM per device.

v0:
```python
from functools import partial
import math

import jax
import jax.numpy as jnp
from jax import lax
from jax.experimental import pallas as pl
from jax.experimental.pallas import tpu as pltpu
from jax.sharding import PartitionSpec as P

D = 5120
HD = 128
TILE = 8
LANES = 128
LEVEL_STEP = 32

EPSILON = 1e-06
MEBI = 1024 * 1024
SMALL = pl.CostEstimate(flops=1, bytes_accessed=1, transcendentals=0)
LARGE = pl.CostEstimate(flops=20_000_000_000, bytes_accessed=1, transcendentals=0)


def kernel_params(limit):
    return pltpu.CompilerParams(vmem_limit_bytes=limit * MEBI)


class Plan:
    def __init__(self, windows, order):
        heads = windows.shape[0]
        self.heads = heads
        self.most = max(heads * 7 // 10, 1)
        self.order = order
        n_ha, n_wa = lax.axis_size("ha"), lax.axis_size("wa")
        ha, wa = lax.axis_index("ha"), lax.axis_index("wa")
        number = lax.broadcasted_iota(jnp.int32, (2, heads, heads), 1)
        other = lax.broadcasted_iota(jnp.int32, (2, heads, heads), 2)
        idle = jnp.where(windows.T > 0, 0, 1)
        before = (idle[:, None, :] < idle[:, :, None]) | (
            (idle[:, None, :] == idle[:, :, None]) & (other < number)
        )
        position = jnp.sum(before.astype(jnp.int32), axis=2)
        sorted_heads = jnp.sum(jnp.where(position[:, None, :] == number, other, 0), axis=2)
        turned = ha if order > 1 else 0 * ha
        edges = jnp.stack([ha > 0, ha < n_ha - 1, wa > 0, wa < n_wa - 1, turned]).astype(jnp.int32)
        self.vector = jnp.concatenate(
            [windows.T.reshape(-1), position.reshape(-1), sorted_heads.reshape(-1), edges]
        )
        self.counts = jnp.sum(1.0 - idle, axis=1)

    def agree(self, counts):
        counts = lax.pmax(counts, "ta")
        self.more_rows = counts[0] > self.most
        self.more_cols = counts[1] > self.most
        return counts

    def row_radius(self, vector, head):
        return vector[head]

    def col_radius(self, vector, head):
        return vector[self.heads + head]

    def row_position(self, vector, head):
        return vector[2 * self.heads + head]

    def col_position(self, vector, head):
        return vector[3 * self.heads + head]

    def row_head(self, vector, position):
        return vector[4 * self.heads + position]

    def col_head(self, vector, position):
        return vector[5 * self.heads + position]

    def edge(self, vector, number):
        return vector[6 * self.heads + number]


def pack_kernel(vector, source, *refs, head_of, first, rows):
    outs, sem = refs[:-1], refs[-1]
    copies = []
    for number, (out, (low, size)) in enumerate(zip(outs, rows)):
        for slot in range(out.shape[-1] // HD):
            start = pl.multiple_of(head_of(vector, first + slot) * HD, HD)
            lead = (slice(None),) * (len(source.shape) - 2)
            copies.append(
                pltpu.make_async_copy(
                    source.at[(*lead, pl.ds(low, size), pl.ds(start, HD))],
                    out.at[(*lead, slice(None), pl.ds(slot * HD, HD))],
                    sem.at[number, slot],
                )
            )
    for copy in copies:
        copy.start()
    for copy in copies:
        copy.wait()


def pack(vector, source, head_of, first, count, rows):
    anywhere = pl.BlockSpec(memory_space=pl.ANY)
    return pl.pallas_call(
        partial(pack_kernel, head_of=head_of, first=first, rows=rows),
        in_specs=[pl.BlockSpec(memory_space=pltpu.SMEM), anywhere],
        out_specs=[pl.BlockSpec(memory_space=pltpu.VMEM)] * len(rows),
        out_shape=[
            jax.ShapeDtypeStruct((*source.shape[:-2], size, count * HD), source.dtype)
            for _, size in rows
        ],
        scratch_shapes=[pltpu.SemaphoreType.DMA((len(rows), count))],
        compiler_params=kernel_params(8),
        cost_estimate=SMALL,
        name="pack",
    )(vector, source)


def attention_kernel(vector, *refs, plan, head_of, q_count, visiting, group):
    q_refs = refs[:q_count]
    kv_ref, top_ref, bottom_ref, top_rest, bottom_rest = refs[q_count : q_count + 5]
    refs = refs[q_count + 5 :]
    out_refs, stat_refs, halo = refs[:q_count], refs[q_count : 2 * q_count], refs[2 * q_count]
    frames, tokens, head_size = q_refs[0].shape
    span = top_ref.shape[2]
    tiles = tokens // span
    step = pl.program_id(0)
    head = head_of(vector, step)
    radius_row = plan.row_radius(vector, head)
    radius_col = plan.col_radius(vector, head)
    scale = 1.0 / math.sqrt(HD)

    @pl.when(step == 0)
    def _():
        for stat_ref in stat_refs:
            stat_ref[...] = jnp.zeros_like(stat_ref)

    def near(which, tile, wide):
        if not wide:
            return kv_ref[which, :, tile * span : (tile + 1) * span, :].reshape(-1, head_size)
        pieces = []
        if tile == 0:
            pieces.append(halo[0, which])
        low = max(tile - 1, 0) * span
        high = min(tile + 2, tiles) * span
        pieces.append(kv_ref[which, :, low:high, :])
        if tile == tiles - 1:
            pieces.append(halo[1, which])
        block = pieces[0] if len(pieces) == 1 else jnp.concatenate(pieces, axis=1)
        return block.reshape(-1, head_size)

    def attend(wide):
        lane = lax.broadcasted_iota(jnp.int32, (frames, span, LANES), 2)
        for tile in range(tiles):
            rows = slice(tile * span, (tile + 1) * span)
            keys = near(0, tile, wide)
            values = near(1, tile, wide)
            bias = None
            if wide and (tile == 0 or tile == tiles - 1):
                place = lax.rem(
                    lax.broadcasted_iota(jnp.int32, (1, keys.shape[0]), 1), 3 * span
                )
                low, high = 0, 3 * span
                if tile == 0:
                    low = jnp.where(plan.edge(vector, 0) == 0, span, 0)
                if tile == tiles - 1:
                    high = jnp.where(plan.edge(vector, 1) == 0, 2 * span, 3 * span)
                bias = jnp.where((place >= low) & (place < high), 0.0, -jnp.inf)
            for q_ref, out_ref, stat_ref in zip(q_refs, out_refs, stat_refs):
                query = q_ref[:, rows, :].reshape(-1, head_size)
                scores = (
                    lax.dot_general(
                        query, keys, (((1,), (1,)), ((), ())), preferred_element_type=jnp.float32
                    )
                    * scale
                )
                if bias is not None:
                    scores = scores + bias
                highest = jnp.max(scores, axis=1, keepdims=True)
                expo = jnp.exp(scores - highest)
                total = jnp.sum(expo, axis=1, keepdims=True)
                output = jnp.dot(
                    expo.astype(jnp.bfloat16), values, preferred_element_type=jnp.float32
                ) * (1.0 / total)
                out_ref[:, rows, :] = output.astype(jnp.bfloat16).reshape(frames, span, head_size)
                level = (highest + jnp.log(total)).reshape(frames, span, 1)
                stat_ref[:, rows, :] = jnp.where(lane == step, level, stat_ref[:, rows, :])

    active = step < group
    if visiting:

        @pl.when(active & (radius_col == 0))
        def _():
            for out_ref in out_refs:
                out_ref[...] = jnp.zeros_like(out_ref)

        active = active & (radius_col != 0)

    @pl.when(active & (radius_row == 0))
    def _():
        attend(False)

    always = plan.row_position(vector, head) < plan.most

    @pl.when(active & (radius_row != 0) & always)
    def _():
        halo[0] = top_ref[...]
        halo[1] = bottom_ref[...]

    @pl.when(active & (radius_row != 0) & jnp.logical_not(always))
    def _():
        halo[0] = top_rest[...]
        halo[1] = bottom_rest[...]

    @pl.when(active & (radius_row != 0))
    def _():
        attend(True)

    @pl.when(step == group)
    def _():
        for out_ref, stat_ref in zip(out_refs, stat_refs):
            level = stat_ref[...]
            high = level.astype(jnp.bfloat16).astype(jnp.float32)
            middle = (level - high).astype(jnp.bfloat16).astype(jnp.float32)
            low = level - high - middle
            packed = high + pltpu.roll(middle, LEVEL_STEP, 2) + pltpu.roll(low, 2 * LEVEL_STEP, 2)
            out_ref[...] = packed.astype(jnp.bfloat16)


def attention(plan, vector, query_blocks, keys_values, halos, first=None):
    frames, tokens, features = query_blocks[0].shape
    group = features // HD
    span = halos[0].shape[2]
    q_count = len(query_blocks)
    visiting = first is not None

    def slot_of(step):
        return jnp.minimum(step, group - 1)

    def head_of(vector, step):
        return plan.col_head(vector, first + slot_of(step)) if visiting else slot_of(step)

    def kv_index(step, vector):
        return 0, 0, 0, head_of(vector, step)

    def halo_index(step, vector):
        position = plan.row_position(vector, head_of(vector, step))
        return 0, 0, 0, jnp.minimum(position, plan.most - 1)

    def rest_index(step, vector):
        position = plan.row_position(vector, head_of(vector, step))
        return 0, 0, 0, jnp.maximum(position - plan.most, 0)

    q_spec = pl.BlockSpec((frames, tokens, HD), lambda step, _: (0, 0, slot_of(step)))
    kv_spec = pl.BlockSpec((2, frames, tokens, HD), kv_index)
    halo_spec = pl.BlockSpec((2, frames, span, HD), halo_index)
    rest_spec = pl.BlockSpec((2, frames, span, HD), rest_index)
    out_spec = pl.BlockSpec((frames, tokens, HD), lambda step, _: (0, 0, step))
    return pl.pallas_call(
        partial(
            attention_kernel,
            plan=plan,
            head_of=head_of,
            q_count=q_count,
            visiting=visiting,
            group=group,
        ),
        grid_spec=pltpu.PrefetchScalarGridSpec(
            num_scalar_prefetch=1,
            grid=(group + 1,),
            in_specs=[q_spec] * q_count + [kv_spec] + [halo_spec] * 2 + [rest_spec] * 2,
            out_specs=[out_spec] * q_count,
            scratch_shapes=[pltpu.VMEM((frames, tokens, LANES), jnp.float32)] * q_count
            + [pltpu.VMEM((2, 2, frames, span, HD), jnp.bfloat16)],
        ),
        out_shape=[jax.ShapeDtypeStruct((frames, tokens, (group + 1) * HD), jnp.bfloat16)]
        * q_count,
        compiler_params=kernel_params(12),
        cost_estimate=SMALL if visiting else LARGE,
        name="attend_visitors" if visiting else "attend_own",
    )(vector, *query_blocks, keys_values, *halos)


def combine_kernel(vector, own, own_stat, left, right, left_rest, right_rest, out, *, plan, heads):
    first = pl.program_id(0) * heads
    frames, tokens, _ = own.shape

    def level(stat, number):
        lane = lax.broadcasted_iota(jnp.int32, (LANES, HD), 0)
        pick = jnp.where(
            (lax.rem(lane, LEVEL_STEP) == number) & (lane < 3 * LEVEL_STEP), 1.0, 0.0
        ).astype(jnp.bfloat16)
        return jnp.dot(
            stat.reshape(-1, LANES), pick, preferred_element_type=jnp.float32
        ).reshape(frames, tokens, HD)

    for index in range(heads):
        head = first + index
        columns = slice(index * HD, (index + 1) * HD)
        across = plan.col_radius(vector, head) != 0
        position = plan.col_position(vector, head)

        @pl.when(jnp.logical_not(across))
        def _(columns=columns):
            out[:, :, columns] = own[:, :, columns]

        def join(sides, slot, columns, head):
            here = pl.ds(pl.multiple_of(slot * HD, HD), HD)
            levels = [level(own_stat[...], head)]
            values = [own[:, :, columns]]
            for number, side in enumerate(sides):
                value = level(side[:, :, side.shape[2] - LANES :], slot)
                levels.append(jnp.where(plan.edge(vector, 2 + number) == 0, -jnp.inf, value))
                values.append(side[:, :, here])
            highest = jnp.maximum(levels[0], jnp.maximum(levels[1], levels[2]))
            weights = [jnp.exp(x - highest) for x in levels]
            mixed = sum(value.astype(jnp.float32) * weight for value, weight in zip(values, weights))
            out[:, :, columns] = (mixed / (weights[0] + weights[1] + weights[2])).astype(
                jnp.bfloat16
            )

        @pl.when(across & (position < plan.most))
        def _(position=position, columns=columns, head=head):
            join((left, right), position, columns, head)

        @pl.when(across & (position >= plan.most))
        def _(position=position, columns=columns, head=head):
            join((left_rest, right_rest), position - plan.most, columns, head)


def combine(plan, vector, near, sides):
    frames, tokens, _ = near.shape
    heads = plan.heads // plan.order
    spec = pl.BlockSpec((frames, tokens, heads * HD), lambda h, _: (0, 0, h))
    stat_spec = pl.BlockSpec((frames, tokens, HD), lambda h, _: (0, 0, plan.heads))
    return pl.pallas_call(
        partial(combine_kernel, plan=plan, heads=heads),
        grid_spec=pltpu.PrefetchScalarGridSpec(
            num_scalar_prefetch=1,
            grid=(plan.order,),
            in_specs=[spec, stat_spec]
            + [pl.BlockSpec(side.shape, lambda h, _: (0, 0, 0)) for side in sides],
            out_specs=pl.BlockSpec(
                (frames, tokens, heads * HD), lambda h, vector: (0, 0, h ^ plan.edge(vector, 4))
            ),
        ),
        out_shape=jax.ShapeDtypeStruct((frames, tokens, plan.heads * HD), jnp.bfloat16),
        compiler_params=kernel_params(18),
        cost_estimate=LARGE,
        name="combine",
    )(vector, near, near, *sides)


def project_kernel(place, attended, *refs, slots, carried, start, column):
    arrays = 1 + max(piece[0] for slot in slots for piece in slot)
    pieces, refs = refs[:arrays], refs[arrays:]
    if carried:
        carry, refs = refs[0], refs[1:]
    out, rows, weight, rows_sem, weight_sem = refs
    columns = weight.shape[1]
    depth = weight.shape[2]
    rows_copy = pltpu.make_async_copy(
        attended.at[:, start : start + depth], rows, rows_sem.at[0]
    )
    rows_copy.start()
    for index, slot in enumerate(slots):
        for block in range(columns):
            low = 0
            for number, (array, size, share, turned) in enumerate(slot):
                first = pl.multiple_of((place[0] ^ share if turned else share) * size, size)
                pltpu.make_async_copy(
                    pieces[array].at[pl.ds(first, size), block * column : (block + 1) * column],
                    weight.at[index, block, low : low + size],
                    weight_sem.at[index, block, number],
                ).start()
                low += size
    rows_copy.wait()
    for index, slot in enumerate(slots):

        def body(block, _, index=index, slot=slot):
            low = 0
            for number, (_, size, _, _) in enumerate(slot):
                piece = weight.at[index, block, low : low + size]
                pltpu.make_async_copy(piece, piece, weight_sem.at[index, block, number]).wait()
                low += size
            total = jnp.dot(rows[...], weight[index, block], preferred_element_type=jnp.float32)
            here = pl.ds(pl.multiple_of(block * column, column), column)
            if carried:
                total = total + carry[index, :, here]
            out[index, :, here] = total.astype(out.dtype)
            return 0

        lax.fori_loop(0, columns, body, 0)


def project(place, attended, arrays, slots, carry, start, dtype):
    tokens = attended.shape[0]
    width = arrays[0].shape[1]
    column = 256 if width % 256 == 0 else width
    columns = width // column
    depth = sum(piece[1] for piece in slots[0])
    held = len(slots) * width * (2 * depth + tokens * jnp.dtype(dtype).itemsize)
    held += tokens * (2 * depth + (0 if carry is None else 4 * len(slots) * width))
    anywhere = pl.BlockSpec(memory_space=pl.ANY)
    inside = pl.BlockSpec(memory_space=pltpu.VMEM)
    return pl.pallas_call(
        partial(
            project_kernel, slots=slots, carried=carry is not None, start=start, column=column
        ),
        in_specs=[pl.BlockSpec(memory_space=pltpu.SMEM), anywhere]
        + [anywhere] * len(arrays)
        + ([] if carry is None else [inside]),
        out_specs=inside,
        out_shape=jax.ShapeDtypeStruct((len(slots), tokens, width), dtype),
        scratch_shapes=[
            pltpu.VMEM((tokens, depth), attended.dtype),
            pltpu.VMEM((len(slots), columns, depth, column), attended.dtype),
            pltpu.SemaphoreType.DMA((1,)),
            pltpu.SemaphoreType.DMA((len(slots), columns, max(len(slot) for slot in slots))),
        ],
        compiler_params=kernel_params(held // MEBI + 3),
        cost_estimate=SMALL,
        name="project",
    )(place, attended, *arrays, *([] if carry is None else [carry]))


def pick_kernel(place, own_hidden, other_hidden, own_gate, other_gate, hidden, gate):
    mine = place[2 * pl.program_id(0)] != 0

    @pl.when(mine)
    def _():
        hidden[0] = own_hidden[...]
        gate[0] = own_gate[...]

    @pl.when(jnp.logical_not(mine))
    def _():
        hidden[0] = other_hidden[...]
        gate[0] = other_gate[...]


def pick(place, own_hidden, other_hidden, own_gate, other_gate, width):
    tokens, features = own_hidden.shape
    count = 2 * features // width
    hidden = pl.BlockSpec((tokens, width), lambda i, place: (0, place[2 * i + 1]))
    gate = pl.BlockSpec((1, width), lambda i, place: (0, place[2 * i + 1]))
    return pl.pallas_call(
        pick_kernel,
        grid_spec=pltpu.PrefetchScalarGridSpec(
            num_scalar_prefetch=1,
            grid=(count,),
            in_specs=[hidden, hidden, gate, gate],
            out_specs=[
                pl.BlockSpec((1, tokens, width), lambda i, place: (i, 0, 0)),
                pl.BlockSpec((1, 1, width), lambda i, place: (i, 0, 0)),
            ],
        ),
        out_shape=[
            jax.ShapeDtypeStruct((count, tokens, width), jnp.bfloat16),
            jax.ShapeDtypeStruct((count, 1, width), jnp.float32),
        ],
        compiler_params=kernel_params(14),
        cost_estimate=SMALL,
        name="pick",
    )(place, own_hidden, other_hidden, own_gate, other_gate)


def mixed_block(hidden, gate, own_part, other_part):
    parts = own_part[0].astype(jnp.float32) + other_part[0].astype(jnp.float32)
    return hidden[0].astype(jnp.float32) + gate * parts


def mix_kernel(hidden, gate, own_part, other_part, mixed_ref, sums_ref):
    mixed = mixed_block(hidden, gate[0], own_part, other_part)
    mixed_ref[0] = mixed.astype(jnp.bfloat16)
    first = jnp.sum(mixed, axis=1, keepdims=True)
    second = jnp.sum(mixed * mixed, axis=1, keepdims=True)
    lane = lax.broadcasted_iota(jnp.int32, sums_ref.shape, 1)
    sums_ref[...] = jnp.where(lane == 0, first, jnp.where(lane == 1, second, 0.0))


def mix(hidden, gate, own_part, other_part):
    _, tokens, width = hidden.shape
    rows = 64 if tokens % 64 == 0 else tokens
    part = pl.BlockSpec((1, rows, width), lambda i: (0, i, 0))
    return pl.pallas_call(
        mix_kernel,
        grid=(tokens // rows,),
        in_specs=[part, pl.BlockSpec(gate.shape, lambda i: (0, 0, 0)), part, part],
        out_specs=[part, pl.BlockSpec((rows, LANES), lambda i: (i, 0))],
        out_shape=[
            jax.ShapeDtypeStruct((1, tokens, width), jnp.bfloat16),
            jax.ShapeDtypeStruct((tokens, LANES), jnp.float32),
        ],
        compiler_params=kernel_params(14),
        cost_estimate=SMALL,
        name="mix",
    )(hidden, gate, own_part, other_part)


def finish_kernel(place, gate, scale, shift_by, sums, early, *refs, count, blocks):
    hidden, own_parts, other_parts = (refs[count * k : count * (k + 1)] for k in range(3))
    residual, ffn = refs[3 * count :]
    width = early.shape[2]
    late = [
        mixed_block(hidden[index], gate[1 + index], own_parts[index], other_parts[index])
        for index in range(count)
    ]
    first = sums[:, 0:1]
    second = sums[:, 1:2]
    for mixed in late:
        first = first + jnp.sum(mixed, axis=1, keepdims=True)
        second = second + jnp.sum(mixed * mixed, axis=1, keepdims=True)
    average = first / D
    variance = second / D - average * average
    inverse = lax.rsqrt(variance + EPSILON)
    for block in range(blocks):
        columns = slice(block * width, (block + 1) * width)
        mixed = early[0].astype(jnp.float32)
        for index in range(count):
            mixed = jnp.where(place[block] == 1 + index, late[index], mixed)
        residual[:, columns] = mixed.astype(jnp.bfloat16)
        ffn[:, columns] = (
            (mixed - average) * inverse * (1.0 + scale[:, columns]) + shift_by[:, columns]
        ).astype(jnp.bfloat16)


def finish(place, hidden, gate, scale, shift_by, sums, early, own_parts, other_parts):
    count = own_parts.shape[0]
    _, tokens, width = hidden.shape
    blocks = place.shape[0]
    rows = 64 if tokens % 64 == 0 else tokens
    part = pl.BlockSpec((1, rows, width), lambda i, place: (0, i, 0))
    whole = pl.BlockSpec((1, blocks * width), lambda i, place: (0, 0))
    row = pl.BlockSpec((rows, blocks * width), lambda i, place: (i, 0))
    parts = [
        pl.BlockSpec((1, rows, width), lambda i, place, index=index: (index, i, 0))
        for index in range(count + 1)
    ]
    return pl.pallas_call(
        partial(finish_kernel, count=count, blocks=blocks),
        grid_spec=pltpu.PrefetchScalarGridSpec(
            num_scalar_prefetch=1,
            grid=(tokens // rows,),
            in_specs=[pl.BlockSpec(gate.shape, lambda i, place: (0, 0, 0)), whole, whole]
            + [pl.BlockSpec((rows, LANES), lambda i, place: (i, 0)), part]
            + parts[1:]
            + parts[:-1] * 2,
            out_specs=[row, row],
        ),
        out_shape=[jax.ShapeDtypeStruct((tokens, blocks * width), jnp.bfloat16)] * 2,
        compiler_params=kernel_params(14),
        cost_estimate=SMALL,
        name="finish",
    )(
        *(place, gate, scale, shift_by, sums, early),
        *([hidden] * count + [own_parts] * count + [other_parts] * count),
    )


def shift(block, axis, step):
    count = lax.axis_size(axis)
    pairs = [(i, i + step) for i in range(count) if 0 <= i + step < count]
    return lax.ppermute(block, axis, pairs)


def turn(block, axis, step):
    count = lax.axis_size(axis)
    return lax.ppermute(block, axis, [(i, (i + step) % count) for i in range(count)])


def swap(block, axis, bit):
    count = lax.axis_size(axis)
    return lax.ppermute(block, axis, [(i, i ^ bit) for i in range(count)])


class Tokens:
    def __init__(self, queries, keys_values, windows, order):
        self.plan = Plan(windows, order)
        self.queries = queries.reshape(queries.shape[0], -1, queries.shape[3])
        self.keys_values = keys_values.reshape(*keys_values.shape[:2], -1, keys_values.shape[4])
        self.span = TILE * queries.shape[2]
        self.parts = (0, self.plan.most), (self.plan.most, self.plan.heads - self.plan.most)

    def edge_rows(self, vector, part):
        low = self.queries.shape[1] - self.span
        rows = [(low, self.span), (0, self.span)]
        return pack(vector, self.keys_values, self.plan.row_head, *self.parts[part], rows)

    def leaving(self, vector, part):
        rows = [(0, self.queries.shape[1])]
        return pack(vector, self.queries, self.plan.col_head, *self.parts[part], rows)[0]

    def halos(self, rows):
        return shift(rows[0], "ha", 1), shift(rows[1], "ha", -1)

    def rest_halos(self, vector):
        shape = (*self.keys_values.shape[:2], self.span, self.parts[1][1] * HD)
        return lax.cond(
            self.plan.more_rows,
            lambda vector: self.halos(self.edge_rows(vector, 1)),
            lambda vector: (jnp.zeros(shape, jnp.bfloat16),) * 2,
            vector,
        )

    def stay(self, vector, halos):
        return attention(self.plan, vector, [self.queries], self.keys_values, halos)[0]

    def visit(self, vector, visitors, halos, part=0):
        first = self.parts[part][0]
        return attention(self.plan, vector, visitors, self.keys_values, halos, first)

    def rest_sides(self, vector, halos):
        shape = (*self.queries.shape[:2], (self.parts[1][1] + 1) * HD)

        def send(vector, *halos):
            queries = self.leaving(vector, 1)
            visitors = shift(queries, "wa", 1), shift(queries, "wa", -1)
            for_left, for_right = self.visit(vector, visitors, halos, 1)
            return shift(for_right, "wa", 1), shift(for_left, "wa", -1)

        return lax.cond(
            self.plan.more_cols,
            send,
            lambda vector, *halos: (jnp.zeros(shape, jnp.bfloat16),) * 2,
            vector,
            *halos,
        )

    def combine(self, vector, near, sides):
        attended = combine(self.plan, vector, near, sides)
        return attended.reshape(-1, attended.shape[2])


def together(*blocks):
    return lax.optimization_barrier(blocks)


def paired(hidden, queries, keys_values, windows, out_weight, picked):
    ha, wa, ta = lax.axis_index("ha"), lax.axis_index("wa"), lax.axis_index("ta")
    n_wa = lax.axis_size("wa")
    blocks = n_wa // 2
    depth = out_weight.shape[0] // 4
    width = out_weight.shape[1]

    def share(shares, number):
        return lax.dynamic_slice_in_dim(shares, number * depth, depth, 0)

    mine = lax.optimization_barrier(share(out_weight, ha))
    first = turn(mine, "wa", 1)
    tokens = Tokens(queries, keys_values, windows, 4)
    vector = tokens.plan.vector
    top, bottom = tokens.halos(tokens.edge_rows(vector, 0))

    top, gate = together(top, picked[0:1])
    other_gate = swap(gate, "ta", 1)
    other_gate, counts = together(other_gate, tokens.plan.counts)
    counts, vector = together(tokens.plan.agree(counts), vector)
    queries, mine = together(tokens.leaving(vector, 0), mine)
    third = turn(mine, "wa", -1)

    first, top, bottom, other_gate, vector, queries = together(
        first, top, bottom, other_gate, vector, queries
    )
    first_x = swap(first, "ha", 1)
    first_y = swap(first, "ha", 2)
    from_left = shift(queries, "wa", 1)
    from_right = shift(queries, "wa", -1)
    halos = top, bottom, *tokens.rest_halos(vector)
    near = tokens.stay(vector, halos)

    rest_sides = tokens.rest_sides(vector, halos)

    near, first_x, first_y, third, first, *rest_sides = together(
        near, first_x, first_y, third, first, *rest_sides
    )
    third_x = swap(third, "ha", 1)
    third_y = swap(third, "ha", 2)
    second = turn(first, "wa", 1)
    for_left, for_right = tokens.visit(vector, (from_left, from_right), halos)

    left = shift(for_right, "wa", 1)
    right = shift(for_left, "wa", -1)

    third_x, third_y, second, vector, hidden, all_shares = together(
        third_x, third_y, second, vector, hidden, out_weight
    )
    second_x = swap(second, "ha", 1)
    second_y = swap(second, "ha", 2)
    other_hidden = swap(hidden, "ta", 1)

    far = lax.optimization_barrier(share(all_shares, ha ^ 3))
    left, right, far = together(left, right, far)
    attended = tokens.combine(vector, near, [left, right, *rest_sides])

    second_x, second_y, first_y, far, attended = together(
        second_x, second_y, first_y, far, attended
    )
    first_far = swap(first_y, "ha", 1)
    second_far = swap(second_x, "ha", 2)
    third_far = turn(far, "wa", -1)

    turned = ha.reshape(1)
    sums = project(
        turned,
        attended,
        [out_weight],
        [[(0, depth, number, True) for number in range(4)]],
        None,
        0,
        jnp.bfloat16,
    )
    other_sums = swap(sums, "ta", 1)
    late = project(
        turned,
        attended,
        [first, first_x, first_y, second, second_x, second_y, third, third_x, third_y],
        [[(start + number, depth, 0, False) for number in range(3)] for start in (0, 3, 6)],
        None,
        0,
        jnp.float32,
    )
    def block_of(distance):
        return lax.rem(wa - distance + n_wa, n_wa)

    owners = jnp.stack([block_of(distance) // blocks == ta for distance in range(n_wa)])
    inner = jnp.stack([lax.rem(block_of(distance), blocks) for distance in range(n_wa)])
    place = jnp.stack([owners.astype(jnp.int32), inner], axis=1).reshape(-1)
    late, place, other_hidden = together(late, place, other_hidden)
    base, gates = pick(place, hidden, other_hidden, gate, other_gate, width)
    early, totals = mix(base, gates, sums, other_sums)

    first_far, second_far, third_far, early, totals, late = together(
        first_far, second_far, third_far, early, totals, late
    )
    late = project(
        turned,
        attended,
        [first_far, second_far, third_far],
        [[(number, depth, 0, False)] for number in range(3)],
        late,
        3 * depth,
        jnp.bfloat16,
    )
    other_late = swap(late, "ta", 1)
    place = jnp.stack(
        [lax.rem(wa - ta * blocks - block + 2 * n_wa, n_wa) for block in range(blocks)]
    )
    return finish(
        place, base, gates, picked[2:3], picked[1:2], totals, early, late, other_late
    )


def gathered(hidden, queries, keys_values, windows, out_weight, picked):
    n_ha, n_wa, n_ta = lax.axis_size("ha"), lax.axis_size("wa"), lax.axis_size("ta")
    ha, ta = lax.axis_index("ha"), lax.axis_index("ta")
    work = Tokens(queries, keys_values, windows, 1)
    vector = work.plan.vector
    work.plan.agree(work.plan.counts)
    halos = *work.halos(work.edge_rows(vector, 0)), *work.rest_halos(vector)
    sent = work.leaving(vector, 0)
    visitors = shift(sent, "wa", 1), shift(sent, "wa", -1)
    near = work.stay(vector, halos)
    for_left, for_right = work.visit(vector, visitors, halos)
    sides = shift(for_right, "wa", 1), shift(for_left, "wa", -1)
    attended = work.combine(vector, near, [*sides, *work.rest_sides(vector, halos)])
    tokens, features = attended.shape
    depth = features // n_ha
    width = out_weight.shape[1]
    share = lax.dynamic_slice_in_dim(out_weight, ha * depth, depth, 0)
    weights = lax.all_gather(share, ("ha", "wa"), axis=0, tiled=False).reshape(
        n_ha, n_wa, depth, width
    )
    partial_sums = jnp.einsum(
        "thk,hwkc->wtc",
        attended.reshape(tokens, n_ha, depth),
        weights,
        preferred_element_type=jnp.float32,
    ).astype(jnp.bfloat16)
    blocks = n_wa // n_ta
    summed = None
    for step in range(n_ta):
        target = lax.rem(ta + step, n_ta)
        piece = lax.dynamic_slice_in_dim(partial_sums, target * blocks, blocks, 0)
        if step:
            piece = turn(piece, "ta", step)
        piece = piece.astype(jnp.float32)
        summed = piece if summed is None else summed + piece
    summed = jnp.transpose(summed, (1, 0, 2)).reshape(tokens, -1)
    mixed = hidden.astype(jnp.float32) + picked[0] * summed
    sum_first, sum_second = lax.psum((jnp.sum(mixed, axis=1), jnp.sum(mixed * mixed, axis=1)), "ta")
    average = (sum_first / D)[:, None]
    variance = (sum_second / D)[:, None] - average * average
    normed = (mixed - average) * lax.rsqrt(variance + EPSILON)
    ffn_input = (normed * (1.0 + picked[2]) + picked[1]).astype(jnp.bfloat16)
    return mixed.astype(jnp.bfloat16), ffn_input


def shards(hidden_states, queries, keys_values, out_weight, mod_table, windows, step_index):
    tokens = math.prod(queries.shape[:3])
    width = hidden_states.shape[3]
    picked = lax.dynamic_index_in_dim(mod_table, step_index[0], 0, keepdims=False)
    sizes = lax.axis_size("ha"), lax.axis_size("wa"), lax.axis_size("ta")
    tuned = sizes == (4, 4, 2) and out_weight.shape[0] % (20 * LANES) == 0
    residual_out, ffn_input = (paired if tuned else gathered)(
        hidden_states.reshape(tokens, width), queries, keys_values, windows, out_weight, picked
    )
    return residual_out.reshape(hidden_states.shape), ffn_input.reshape(hidden_states.shape)


def solution(mesh):
    return jax.shard_map(
        shards,
        mesh=mesh,
        in_specs=(
            P(None, "ha", "wa", "ta"),
            P(None, "ha", "wa", "ta"),
            P(None, None, "ha", "wa", "ta"),
            P("ta", "wa"),
            P(None, None, "ta"),
            P("ta", None),
            P(),
        ),
        out_specs=(P(None, "ha", "wa", "ta"), P(None, "ha", "wa", "ta")),
        check_vma=False,
    )
```

profile of v0, /device:TPU:0, one launch (start us, length us, event | category | flops | bytes accessed | tf_op | source)
XLA Modules:
  0.0 252.6 jit_solution(7307404483730164236)
XLA Ops:
  3.4 3.0 %collective-permute-start.6 = (bf16[640,1280]{1,0:T(8,128)(2,1)}, bf16[640,1280]{1,0:T(8,128)(2,1)S(1)}, u32[]{:S(2)}, u32[]{:S(2)}) collective-permute-start(bf16[640,1280]{1,0:T(8,128)(2,1)} %constant_dynamic-slice_fusion.1), channel_id=1, source_target_pairs={{0,2},{2,4},{4,6},{6,0},{1,3},{3,5},{5,7},{7,1},{8,10},{10,12},{12... | collective-permute-start | bytes 4915208 | tf_op jit(solution)/shard_map/ppermute | solution.py:564
  7.9 3.3 %pack.6 = (bf16[2,2,64,1792]{3,2,1,0:T(8,128)(2,1)S(1)}, bf16[2,2,64,1792]{3,2,1,0:T(8,128)(2,1)}) custom-call(s32[125]{0:T(128)S(1)} %concatenate.10.vector, bf16[2,2,192,2560]{3,2,1,0:T(8,128)(2,1)} %bitcast.44), custom_call_target="tpu_custom_call" | custom-call | flops 1 | bytes 1 | tf_op jit(solution)/shard_map/pack/pallas_call | solution.py:100
  11.2 3.5 %collective-permute-start.7 = (bf16[2,2,64,1792]{3,2,1,0:T(8,128)(2,1)S(1)}, bf16[2,2,64,1792]{3,2,1,0:T(8,128)(2,1)S(1)}, u32[]{:S(2)}, u32[]{:S(2)}) collective-permute-start(bf16[2,2,64,1792]{3,2,1,0:T(8,128)(2,1)S(1)} %get-tuple-element.90), channel_id=1, source_target_pairs={{0,8},{8,16},{16,24},{1,9},{9,17},{17,25},{2,10},{10,18},{18,26},{... | collective-permute-start | bytes 2752520 | tf_op jit(solution)/shard_map/ppermute | solution.py:559
  17.7 16.3 %collective-permute-done.7.refs_2_.refs_3_ = bf16[2,2,64,1792]{3,2,1,0:T(8,128)(2,1)S(1)} collective-permute-done((bf16[2,2,64,1792]{3,2,1,0:T(8,128)(2,1)S(1)}, bf16[2,2,64,1792]{3,2,1,0:T(8,128)(2,1)S(1)}, u32[]{:S(2)}, u32[]{:S(2)}) %collective-permute-start.7) | collective-permute-done | bytes 917536 | tf_op jit(solution)/shard_map/ppermute | solution.py:559
  37.6 3.2 %pack.7 = bf16[2,192,1792]{2,1,0:T(8,128)(2,1)} custom-call(s32[125]{0:T(128)S(1)} %concatenate.10.vector, bf16[2,192,2560]{2,1,0:T(8,128)(2,1)} %bitcast.49), custom_call_target="tpu_custom_call" | custom-call | flops 1 | bytes 1 | tf_op jit(solution)/shard_map/pack/pallas_call | solution.py:100
  44.8 10.9 %collective-permute-done.8.refs_3_.refs_4_ = bf16[2,2,64,1792]{3,2,1,0:T(8,128)(2,1)} collective-permute-done((bf16[2,2,64,1792]{3,2,1,0:T(8,128)(2,1)}, bf16[2,2,64,1792]{3,2,1,0:T(8,128)(2,1)}, u32[]{:S(2)}, u32[]{:S(2)}) %collective-permute-start.8) | collective-permute-done | bytes 917536 | tf_op jit(solution)/shard_map/ppermute | solution.py:559
  57.0 5.6 %collective-permute-start.18 = (bf16[2,192,1792]{2,1,0:T(8,128)(2,1)}, bf16[2,192,1792]{2,1,0:T(8,128)(2,1)}, u32[]{:S(2)}, u32[]{:S(2)}) collective-permute-start(bf16[2,192,1792]{2,1,0:T(8,128)(2,1)} %pack.7), channel_id=1, source_target_pairs={{0,2},{2,4},{4,6},{1,3},{3,5},{5,7},{8,10},{10,12},{12,14},{9,11},... | collective-permute-start | bytes 4128776 | tf_op jit(solution)/shard_map/ppermute | solution.py:559
  67.5 22.9 %attend_own.1.own.own_stat = bf16[2,192,2688]{2,1,0:T(8,128)(2,1)S(1)} custom-call(s32[125]{0:T(128)S(1)} %concatenate.10.vector, bf16[2,192,2560]{2,1,0:T(8,128)(2,1)} %bitcast.51, bf16[2,2,192,2560]{3,2,1,0:T(8,128)(2,1)} %bitcast.47, bf16[2,2,64,1792]{3,2,1,0:T(8,128)(2,1)} %copy-done.17, bf16[2,2,64,1792]{3,2,1,0:T(8,128)(2,1)} %collective-permute-done.8.refs_3_.refs_4_, ...), custom_call_target="tpu_custom_call" | custom-call | flops 20000000000 | bytes 1 | tf_op jit(solution)/shard_map/attend_own/pallas_call | solution.py:255
  91.8 10.1 %collective-permute-done.11.refs_2_ = bf16[640,1280]{1,0:T(8,128)(2,1)} collective-permute-done((bf16[640,1280]{1,0:T(8,128)(2,1)S(1)}, bf16[640,1280]{1,0:T(8,128)(2,1)}, u32[]{:S(2)}, u32[]{:S(2)}) %collective-permute-start.11) | collective-permute-done | bytes 1638432 | tf_op jit(solution)/shard_map/ppermute | solution.py:569
  106.7 3.5 %collective-permute-done.19.refs_1_ = bf16[2,192,1792]{2,1,0:T(8,128)(2,1)} collective-permute-done((bf16[2,192,1792]{2,1,0:T(8,128)(2,1)}, bf16[2,192,1792]{2,1,0:T(8,128)(2,1)}, u32[]{:S(2)}, u32[]{:S(2)}) %collective-permute-start.19) | collective-permute-done | bytes 1376288 | tf_op jit(solution)/shard_map/ppermute | solution.py:559
  110.9 25.9 %attend_visitors.3 = (bf16[2,192,1920]{2,1,0:T(8,128)(2,1)}, bf16[2,192,1920]{2,1,0:T(8,128)(2,1)}) custom-call(s32[125]{0:T(128)S(1)} %concatenate.10.vector, bf16[2,192,1792]{2,1,0:T(8,128)(2,1)} %collective-permute-done.18.refs_0_, bf16[2,192,1792]{2,1,0:T(8,128)(2,1)} %collective-permute-done.19.refs_1_, bf16[2,2,192,2560]{3,2,1,0:T(8,128)(2,1)S(1)} %bitcast.48, ...), custom_call_target="tpu_custom_call" | custom-call | flops 1 | bytes 1 | tf_op jit(solution)/shard_map/attend_visitors/pallas_call | solution.py:255
  136.8 5.5 %collective-permute-start.20 = (bf16[2,192,1920]{2,1,0:T(8,128)(2,1)}, bf16[2,192,1920]{2,1,0:T(8,128)(2,1)}, u32[]{:S(2)}, u32[]{:S(2)}) collective-permute-start(bf16[2,192,1920]{2,1,0:T(8,128)(2,1)} %get-tuple-element.112), channel_id=1, source_target_pairs={{0,2},{2,4},{4,6},{1,3},{3,5},{5,7},{8,10},{10,12},{12,14},{9,11},... | collective-permute-start | bytes 4423688 | tf_op jit(solution)/shard_map/ppermute | solution.py:559
  143.8 4.3 %collective-permute-done.15.refs_3_ = bf16[640,1280]{1,0:T(8,128)(2,1)} collective-permute-done((bf16[640,1280]{1,0:T(8,128)(2,1)S(1)}, bf16[640,1280]{1,0:T(8,128)(2,1)}, u32[]{:S(2)}, u32[]{:S(2)}) %collective-permute-start.15) | collective-permute-done | bytes 1638432 | tf_op jit(solution)/shard_map/ppermute | solution.py:564
  148.1 4.9 %collective-permute-start.17 = (bf16[640,1280]{1,0:T(8,128)(2,1)}, bf16[640,1280]{1,0:T(8,128)(2,1)S(1)}, u32[]{:S(2)}, u32[]{:S(2)}) collective-permute-start(bf16[640,1280]{1,0:T(8,128)(2,1)} %collective-permute-done.15.refs_3_), channel_id=1, source_target_pairs={{0,16},{8,24},{16,0},{24,8},{1,17},{9,25},{17,1},{25,9},{2,18},{10... | collective-permute-start | bytes 4915208 | tf_op jit(solution)/shard_map/ppermute | solution.py:569
  153.7 2.8 %constant_dynamic-slice_fusion = bf16[640,1280]{1,0:T(8,128)(2,1)} fusion(bf16[2560,1280]{1,0:T(8,128)(2,1)} %refs_0_.1, s32[]{:T(128)S(6)} %select_n.36), kind=kLoop, calls=%fused_computation.9 | loop fusion | bytes 3276804 | tf_op jit(solution)/shard_map/dynamic_slice | solution.py:642
  156.5 20.3 %collective-permute-done.20.left = bf16[2,192,1920]{2,1,0:T(8,128)(2,1)} collective-permute-done((bf16[2,192,1920]{2,1,0:T(8,128)(2,1)}, bf16[2,192,1920]{2,1,0:T(8,128)(2,1)}, u32[]{:S(2)}, u32[]{:S(2)}) %collective-permute-start.20) | collective-permute-done | bytes 1474592 | tf_op jit(solution)/shard_map/ppermute | solution.py:559
  178.9 7.9 %combine.1 = bf16[2,192,2560]{2,1,0:T(8,128)(2,1)S(1)} custom-call(s32[125]{0:T(128)S(1)} %concatenate.10.vector, bf16[2,192,2688]{2,1,0:T(8,128)(2,1)S(1)} %copy-done.15, bf16[2,192,2688]{2,1,0:T(8,128)(2,1)S(1)} %copy-done.15, bf16[2,192,1920]{2,1,0:T(8,128)(2,1)} %collective-permute-done.20.left, bf16[2,192,1920]{2,1,0:T(8,128)(2,1)} %collective-permute-done.21.right, ...), custom_call_target="tpu_custom_call" | custom-call | flops 20000000000 | bytes 1 | tf_op jit(solution)/shard_map/combine/pallas_call | solution.py:332
  194.5 4.5 %project.4.own_part = bf16[1,384,1280]{2,1,0:T(8,128)(2,1)S(1)} custom-call(s32[1]{0:T(128)} %bitcast.2.place, bf16[384,2560]{1,0:T(8,128)(2,1)S(1)} %bitcast.39, bf16[2560,1280]{1,0:T(8,128)(2,1)S(1)} %bitcast.43), custom_call_target="tpu_custom_call" | custom-call | flops 1 | bytes 1 | tf_op jit(solution)/shard_map/project/pallas_call | solution.py:402
  205.3 10.2 %project.3.refs_3_ = f32[3,384,1280]{2,1,0:T(8,128)S(1)} custom-call(s32[1]{0:T(128)} %bitcast.2.place, bf16[384,2560]{1,0:T(8,128)(2,1)S(1)} %bitcast.40, bf16[640,1280]{1,0:T(8,128)(2,1)S(1)} %copy-done.5, bf16[640,1280]{1,0:T(8,128)(2,1)S(1)} %copy-done.9, bf16[640,1280]{1,0:T(8,128)(2,1)} %collective-permute-done.11.refs_2_, ...), custom_call_target="tpu_custom_call" | custom-call | flops 1 | bytes 1 | tf_op jit(solution)/shard_map/project/pallas_call | solution.py:402
  215.5 4.4 %pick.1 = (bf16[4,384,1280]{2,1,0:T(8,128)(2,1)S(1)}, f32[4,1,1280]{2,1,0:T(1,128)S(1)}) custom-call(s32[8]{0:T(128)S(1)} %reshape.118.place, bf16[384,2560]{1,0:T(8,128)(2,1)} %bitcast.14.own_hidden, bf16[384,2560]{1,0:T(8,128)(2,1)} %collective-permute-done.22.other_hidden, f32[1,2560]{1,0:T(1,128)S(1)} %get-tuple-element.93.own_gate, ...), custom_call_target="tpu_custom_call" | custom-call | flops 1 | bytes 1 | tf_op jit(solution)/shard_map/pick/pallas_call | solution.py:442
  220.0 4.6 %mix.1 = (bf16[1,384,1280]{2,1,0:T(8,128)(2,1)S(1)}, f32[384,128]{1,0:T(8,128)S(1)}) custom-call(bf16[4,384,1280]{2,1,0:T(8,128)(2,1)S(1)} %get-tuple-element.135.hidden.refs_0_.refs_1_.refs_2_, f32[4,1,1280]{2,1,0:T(1,128)S(1)} %get-tuple-element.133.gate, bf16[1,384,1280]{2,1,0:T(8,128)(2,1)S(1)} %project.4.own_part, ...), custom_call_target="tpu_custom_call" | custom-call | flops 1 | bytes 1 | tf_op jit(solution)/shard_map/mix/pallas_call | solution.py:481
  230.1 6.0 %project.5.refs_3_.refs_4_.refs_5_ = bf16[3,384,1280]{2,1,0:T(8,128)(2,1)S(1)} custom-call(s32[1]{0:T(128)} %bitcast.2.place, bf16[384,2560]{1,0:T(8,128)(2,1)S(1)} %bitcast.41, bf16[640,1280]{1,0:T(8,128)(2,1)} %collective-permute-done.23.refs_0_, bf16[640,1280]{1,0:T(8,128)(2,1)} %collective-permute-done.24.refs_1_, ...), custom_call_target="tpu_custom_call" | custom-call | flops 1 | bytes 1 | tf_op jit(solution)/shard_map/project/pallas_call | solution.py:402
  236.2 5.4 %collective-permute-done.27.refs_6_.refs_7_.refs_8_ = bf16[3,384,1280]{2,1,0:T(8,128)(2,1)} collective-permute-done((bf16[3,384,1280]{2,1,0:T(8,128)(2,1)S(1)}, bf16[3,384,1280]{2,1,0:T(8,128)(2,1)}, u32[]{:S(2)}, u32[]{:S(2)}) %collective-permute-start.27) | collective-permute-done | bytes 2949152 | tf_op jit(solution)/shard_map/ppermute | solution.py:569
  245.0 7.6 %finish.1 = (bf16[384,2560]{1,0:T(8,128)(2,1)}, bf16[384,2560]{1,0:T(8,128)(2,1)}) custom-call(s32[2]{0:T(128)S(1)} %pad_add_fusion.1.place, f32[4,1,1280]{2,1,0:T(1,128)S(1)} %get-tuple-element.133.gate, f32[1,2560]{1,0:T(1,128)S(1)} %get-tuple-element.148.scale, f32[1,2560]{1,0:T(1,128)S(1)} %get-tuple-element.147.shift_by, ...), custom_call_target="tpu_custom_call" | custom-call | flops 1 | bytes 1 | tf_op jit(solution)/shard_map/finish/pallas_call | solution.py:535
  (104 shorter events, 56.4 us)
Async XLA Ops:
  3.4 52.3 %collective-permute-start.6 = (bf16[640,1280]{1,0:T(8,128)(2,1)}, bf16[640,1280]{1,0:T(8,128)(2,1)S(1)}, u32[]{:S(2)}, u32[]{:S(2)}) collective-permute-start(bf16[640,1280]{1,0:T(8,128)(2,1)} %constant_dynamic-slice_fusion.1), channel_id=1, source_target_pairs={{0,2},{2,4},{4,6},{6,0},{1,3},{3,5},{5,7},{7,1},{8,10},{10,12},{12... | collective-permute-start | bytes 4915208 | tf_op jit(solution)/shard_map/ppermute | solution.py:564
  11.2 22.7 %collective-permute-start.7 = (bf16[2,2,64,1792]{3,2,1,0:T(8,128)(2,1)S(1)}, bf16[2,2,64,1792]{3,2,1,0:T(8,128)(2,1)S(1)}, u32[]{:S(2)}, u32[]{:S(2)}) collective-permute-start(bf16[2,2,64,1792]{3,2,1,0:T(8,128)(2,1)S(1)} %get-tuple-element.90), channel_id=1, source_target_pairs={{0,8},{8,16},{16,24},{1,9},{9,17},{17,25},{2,10},{10,18},{18,26},{... | collective-permute-start | bytes 2752520 | tf_op jit(solution)/shard_map/ppermute | solution.py:559
  14.7 41.0 %collective-permute-start.8 = (bf16[2,2,64,1792]{3,2,1,0:T(8,128)(2,1)}, bf16[2,2,64,1792]{3,2,1,0:T(8,128)(2,1)}, u32[]{:S(2)}, u32[]{:S(2)}) collective-permute-start(bf16[2,2,64,1792]{3,2,1,0:T(8,128)(2,1)} %get-tuple-element.92), channel_id=1, source_target_pairs={{8,0},{16,8},{24,16},{9,1},{17,9},{25,17},{10,2},{18,10},{26,18},{... | collective-permute-start | bytes 2752520 | tf_op jit(solution)/shard_map/ppermute | solution.py:559
  34.0 1.2 collective-permute-start.9
  42.5 49.3 %collective-permute-start.12 = (bf16[640,1280]{1,0:T(8,128)(2,1)}, bf16[640,1280]{1,0:T(8,128)(2,1)S(1)}, u32[]{:S(2)}, u32[]{:S(2)}) collective-permute-start(bf16[640,1280]{1,0:T(8,128)(2,1)} %constant_dynamic-slice_fusion.1), channel_id=1, source_target_pairs={{0,6},{2,0},{4,2},{6,4},{1,7},{3,1},{5,3},{7,5},{8,14},{10,8},{12,... | collective-permute-start | bytes 4915208 | tf_op jit(solution)/shard_map/ppermute | solution.py:564
  55.7 47.4 %copy-start.4 = (bf16[640,1280]{1,0:T(8,128)(2,1)}, bf16[640,1280]{1,0:T(8,128)(2,1)S(1)}, u32[]{:S(2)}) copy-start(bf16[640,1280]{1,0:T(8,128)(2,1)S(1)} %collective-permute-done.6.refs_0_) | copy-start | bytes 4915204
  55.7 54.5 %collective-permute-start.19 = (bf16[2,192,1792]{2,1,0:T(8,128)(2,1)}, bf16[2,192,1792]{2,1,0:T(8,128)(2,1)}, u32[]{:S(2)}, u32[]{:S(2)}) collective-permute-start(bf16[2,192,1792]{2,1,0:T(8,128)(2,1)} %pack.7), channel_id=1, source_target_pairs={{2,0},{4,2},{6,4},{3,1},{5,3},{7,5},{10,8},{12,10},{14,12},{11,9},... | collective-permute-start | bytes 4128776 | tf_op jit(solution)/shard_map/ppermute | solution.py:559
  57.0 53.9 %collective-permute-start.18 = (bf16[2,192,1792]{2,1,0:T(8,128)(2,1)}, bf16[2,192,1792]{2,1,0:T(8,128)(2,1)}, u32[]{:S(2)}, u32[]{:S(2)}) collective-permute-start(bf16[2,192,1792]{2,1,0:T(8,128)(2,1)} %pack.7), channel_id=1, source_target_pairs={{0,2},{2,4},{4,6},{1,3},{3,5},{5,7},{8,10},{10,12},{12,14},{9,11},... | collective-permute-start | bytes 4128776 | tf_op jit(solution)/shard_map/ppermute | solution.py:559
  66.0 35.9 %collective-permute-start.11 = (bf16[640,1280]{1,0:T(8,128)(2,1)S(1)}, bf16[640,1280]{1,0:T(8,128)(2,1)}, u32[]{:S(2)}, u32[]{:S(2)}) collective-permute-start(bf16[640,1280]{1,0:T(8,128)(2,1)S(1)} %collective-permute-done.6.refs_0_), channel_id=1, source_target_pairs={{0,16},{8,24},{16,0},{24,8},{1,17},{9,25},{17,1},{25,9},{2,18},{10... | collective-permute-start | bytes 4915208 | tf_op jit(solution)/shard_map/ppermute | solution.py:569
  66.0 35.9 %collective-permute-start.10 = (bf16[640,1280]{1,0:T(8,128)(2,1)S(1)}, bf16[640,1280]{1,0:T(8,128)(2,1)S(1)}, u32[]{:S(2)}, u32[]{:S(2)}) collective-permute-start(bf16[640,1280]{1,0:T(8,128)(2,1)S(1)} %collective-permute-done.6.refs_0_), channel_id=1, source_target_pairs={{0,8},{8,0},{16,24},{24,16},{1,9},{9,1},{17,25},{25,17},{2,10},{10... | collective-permute-start | bytes 4915208 | tf_op jit(solution)/shard_map/ppermute | solution.py:569
  91.8 45.1 %copy-start.6 = (bf16[640,1280]{1,0:T(8,128)(2,1)}, bf16[640,1280]{1,0:T(8,128)(2,1)S(1)}, u32[]{:S(2)}) copy-start(bf16[640,1280]{1,0:T(8,128)(2,1)S(1)} %collective-permute-done.12.refs_6_) | copy-start | bytes 4915204
  103.1 45.1 %collective-permute-start.15 = (bf16[640,1280]{1,0:T(8,128)(2,1)S(1)}, bf16[640,1280]{1,0:T(8,128)(2,1)}, u32[]{:S(2)}, u32[]{:S(2)}) collective-permute-start(bf16[640,1280]{1,0:T(8,128)(2,1)S(1)} %collective-permute-done.6.refs_0_), channel_id=1, source_target_pairs={{0,2},{2,4},{4,6},{6,0},{1,3},{3,5},{5,7},{7,1},{8,10},{10,12},{12... | collective-permute-start | bytes 4915208 | tf_op jit(solution)/shard_map/ppermute | solution.py:564
  103.6 44.6 %collective-permute-start.14 = (bf16[640,1280]{1,0:T(8,128)(2,1)S(1)}, bf16[640,1280]{1,0:T(8,128)(2,1)}, u32[]{:S(2)}, u32[]{:S(2)}) collective-permute-start(bf16[640,1280]{1,0:T(8,128)(2,1)S(1)} %collective-permute-done.12.refs_6_), channel_id=1, source_target_pairs={{0,16},{8,24},{16,0},{24,8},{1,17},{9,25},{17,1},{25,9},{2,18},{10... | collective-permute-start | bytes 4915208 | tf_op jit(solution)/shard_map/ppermute | solution.py:569
  105.2 42.9 %collective-permute-start.13 = (bf16[640,1280]{1,0:T(8,128)(2,1)S(1)}, bf16[640,1280]{1,0:T(8,128)(2,1)}, u32[]{:S(2)}, u32[]{:S(2)}) collective-permute-start(bf16[640,1280]{1,0:T(8,128)(2,1)S(1)} %collective-permute-done.12.refs_6_), channel_id=1, source_target_pairs={{0,8},{8,0},{16,24},{24,16},{1,9},{9,1},{17,25},{25,17},{2,10},{10... | collective-permute-start | bytes 4915208 | tf_op jit(solution)/shard_map/ppermute | solution.py:569
  136.8 40.0 %collective-permute-start.20 = (bf16[2,192,1920]{2,1,0:T(8,128)(2,1)}, bf16[2,192,1920]{2,1,0:T(8,128)(2,1)}, u32[]{:S(2)}, u32[]{:S(2)}) collective-permute-start(bf16[2,192,1920]{2,1,0:T(8,128)(2,1)} %get-tuple-element.112), channel_id=1, source_target_pairs={{0,2},{2,4},{4,6},{1,3},{3,5},{5,7},{8,10},{10,12},{12,14},{9,11},... | collective-permute-start | bytes 4423688 | tf_op jit(solution)/shard_map/ppermute | solution.py:559
  142.4 36.6 %collective-permute-start.21 = (bf16[2,192,1920]{2,1,0:T(8,128)(2,1)}, bf16[2,192,1920]{2,1,0:T(8,128)(2,1)}, u32[]{:S(2)}, u32[]{:S(2)}) collective-permute-start(bf16[2,192,1920]{2,1,0:T(8,128)(2,1)} %get-tuple-element.113), channel_id=1, source_target_pairs={{2,0},{4,2},{6,4},{3,1},{5,3},{7,5},{10,8},{12,10},{14,12},{11,9},... | collective-permute-start | bytes 4423688 | tf_op jit(solution)/shard_map/ppermute | solution.py:559
  148.1 39.7 %collective-permute-start.17 = (bf16[640,1280]{1,0:T(8,128)(2,1)}, bf16[640,1280]{1,0:T(8,128)(2,1)S(1)}, u32[]{:S(2)}, u32[]{:S(2)}) collective-permute-start(bf16[640,1280]{1,0:T(8,128)(2,1)} %collective-permute-done.15.refs_3_), channel_id=1, source_target_pairs={{0,16},{8,24},{16,0},{24,8},{1,17},{9,25},{17,1},{25,9},{2,18},{10... | collective-permute-start | bytes 4915208 | tf_op jit(solution)/shard_map/ppermute | solution.py:569
  153.1 36.3 %collective-permute-start.16 = (bf16[640,1280]{1,0:T(8,128)(2,1)}, bf16[640,1280]{1,0:T(8,128)(2,1)}, u32[]{:S(2)}, u32[]{:S(2)}) collective-permute-start(bf16[640,1280]{1,0:T(8,128)(2,1)} %collective-permute-done.15.refs_3_), channel_id=1, source_target_pairs={{0,8},{8,0},{16,24},{24,16},{1,9},{9,1},{17,25},{25,17},{2,10},{10... | collective-permute-start | bytes 4915208 | tf_op jit(solution)/shard_map/ppermute | solution.py:569
  178.9 36.6 %collective-permute-start.22 = (bf16[384,2560]{1,0:T(8,128)(2,1)}, bf16[384,2560]{1,0:T(8,128)(2,1)}, u32[]{:S(2)}, u32[]{:S(2)}) collective-permute-start(bf16[384,2560]{1,0:T(8,128)(2,1)} %bitcast.14.own_hidden), channel_id=1, source_target_pairs={{0,1},{1,0},{2,3},{3,2},{4,5},{5,4},{6,7},{7,6},{8,9},{9,8},{10,11... | collective-permute-start | bytes 5898248 | tf_op jit(solution)/shard_map/ppermute | solution.py:569
  189.4 37.0 %collective-permute-start.25 = (bf16[640,1280]{1,0:T(8,128)(2,1)}, bf16[640,1280]{1,0:T(8,128)(2,1)}, u32[]{:S(2)}, u32[]{:S(2)}) collective-permute-start(bf16[640,1280]{1,0:T(8,128)(2,1)} %constant_dynamic-slice_fusion), channel_id=1, source_target_pairs={{0,6},{2,0},{4,2},{6,4},{1,7},{3,1},{5,3},{7,5},{8,14},{10,8},{12,... | collective-permute-start | bytes 4915208 | tf_op jit(solution)/shard_map/ppermute | solution.py:564
  192.2 36.5 %collective-permute-start.23 = (bf16[640,1280]{1,0:T(8,128)(2,1)}, bf16[640,1280]{1,0:T(8,128)(2,1)}, u32[]{:S(2)}, u32[]{:S(2)}) collective-permute-start(bf16[640,1280]{1,0:T(8,128)(2,1)} %collective-permute-done.11.refs_2_), channel_id=1, source_target_pairs={{0,8},{8,0},{16,24},{24,16},{1,9},{9,1},{17,25},{25,17},{2,10},{10... | collective-permute-start | bytes 4915208 | tf_op jit(solution)/shard_map/ppermute | solution.py:569
  192.7 37.3 %collective-permute-start.24 = (bf16[640,1280]{1,0:T(8,128)(2,1)}, bf16[640,1280]{1,0:T(8,128)(2,1)}, u32[]{:S(2)}, u32[]{:S(2)}) collective-permute-start(bf16[640,1280]{1,0:T(8,128)(2,1)} %collective-permute-done.16.refs_4_), channel_id=1, source_target_pairs={{0,16},{8,24},{16,0},{24,8},{1,17},{9,25},{17,1},{25,9},{2,18},{10... | collective-permute-start | bytes 4915208 | tf_op jit(solution)/shard_map/ppermute | solution.py:569
  199.0 21.0 %collective-permute-start.26 = (bf16[1,384,1280]{2,1,0:T(8,128)(2,1)S(1)}, bf16[1,384,1280]{2,1,0:T(8,128)(2,1)}, u32[]{:S(2)}, u32[]{:S(2)}) collective-permute-start(bf16[1,384,1280]{2,1,0:T(8,128)(2,1)S(1)} %project.4.own_part), channel_id=1, source_target_pairs={{0,1},{1,0},{2,3},{3,2},{4,5},{5,4},{6,7},{7,6},{8,9},{9,8},{10,11... | collective-permute-start | bytes 2949128 | tf_op jit(solution)/shard_map/ppermute | solution.py:569
  236.1 5.6 %collective-permute-start.27 = (bf16[3,384,1280]{2,1,0:T(8,128)(2,1)S(1)}, bf16[3,384,1280]{2,1,0:T(8,128)(2,1)}, u32[]{:S(2)}, u32[]{:S(2)}) collective-permute-start(bf16[3,384,1280]{2,1,0:T(8,128)(2,1)S(1)} %project.5.refs_3_.refs_4_.refs_5_), channel_id=1, source_target_pairs={{0,1},{1,0},{2,3},{3,2},{4,5},{5,4},{6,7},{7,6},{8,9},{9,8},{10,11... | collective-permute-start | bytes 8847368 | tf_op jit(solution)/shard_map/ppermute | solution.py:569
  (20 other events, 261.5 us)
where the time goes:
time: 254 us; the launch traced here: 253 us
  Pallas kernels  101 us (40%)
  waiting for transfers between devices  81.7 us (32%)
  starting transfers between devices  40 us (16%)
  local copies, waits for them, and re-layouts  23.9 us (9%)
  between operations  2.81 us (1%)
    ppermute x6, waiting for transfers between devices, shift(): return lax.ppermute(block, axis, pairs)  53.7 us
    pallas_call x2, Pallas kernels, attention(): pl.pallas_call(partial(attention_kernel, plan=plan, head_of=head_of, q_co...  48.9 us
    ppermute x12, waiting for transfers between devices, swap(): return lax.ppermute(block, axis, [(i, i ^ bit) for i in range(count)])  22.8 us
    pallas_call x3, Pallas kernels, project(): pl.pallas_call(partial(project_kernel, slots=slots, carried=carry is not...  20.7 us
    ppermute x6, starting transfers between devices, shift(): return lax.ppermute(block, axis, pairs)  18.7 us
    ppermute x12, starting transfers between devices, swap(): return lax.ppermute(block, axis, [(i, i ^ bit) for i in range(count)])  12.6 us
    unnamed x44, local copies, waits for them, and re-layouts  12.6 us
    ppermute x4, starting transfers between devices, turn(): lax.ppermute(block, axis, [(i, (i + step) % count) for i in range(count)])  8.64 us
  transfers between devices with their start and end apart: 22, of which 15 were waited for; matrix products, arithmetic and copies ran while one was open for 4% of the time, Pallas kernels for 34%

commit v1 on v0

--- a/solution.py
+++ b/solution.py
@@ -28,7 +28,7 @@
     def __init__(self, windows, order):
         heads = windows.shape[0]
         self.heads = heads
-        self.most = max(heads * 7 // 10, 1)
+        self.most = max(heads * 3 // 4, 1)
         self.order = order
         n_ha, n_wa = lax.axis_size("ha"), lax.axis_size("wa")
         ha, wa = lax.axis_index("ha"), lax.axis_index("wa")

time: 254 us -> 260 us (1.024)
  the two profiles are of different devices: /device:TPU:0 before, /device:TPU:17 now
where the time goes in v1:
time: 260 us; the launch traced here: 255 us
  Pallas kernels  101 us (39%)
  waiting for transfers between devices  85.4 us (33%)
  starting transfers between devices  38.9 us (15%)
  local copies, waits for them, and re-layouts  23.8 us (9%)
  between operations  2.82 us (1%)
    ppermute x6, waiting for transfers between devices, shift(): return lax.ppermute(block, axis, pairs)  63.8 us
    pallas_call x2, Pallas kernels, attention(): pl.pallas_call(partial(attention_kernel, plan=plan, head_of=head_of, q_co...  48.9 us
    pallas_call x3, Pallas kernels, project(): pl.pallas_call(partial(project_kernel, slots=slots, carried=carry is not...  20.7 us
    ppermute x12, starting transfers between devices, swap(): return lax.ppermute(block, axis, [(i, i ^ bit) for i in range(count)])  19.5 us
    ppermute x12, waiting for transfers between devices, swap(): return lax.ppermute(block, axis, [(i, i ^ bit) for i in range(count)])  18.2 us
    ppermute x6, starting transfers between devices, shift(): return lax.ppermute(block, axis, pairs)  17.2 us
    unnamed x40, local copies, waits for them, and re-layouts  12.6 us
    pallas_call x1, Pallas kernels, combine(): pl.pallas_call(partial(combine_kernel, plan=plan, heads=heads), grid_spec...  7.91 us
  transfers between devices with their start and end apart: 22, of which 11 were waited for; matrix products, arithmetic and copies ran while one was open for 4% of the time, Pallas kernels for 34%

profile of v1, /device:TPU:17, one launch (start us, length us, event | category | flops | bytes accessed | tf_op | source)
XLA Modules:
  0.0 255.5 jit_solution(8330673896676292126)
XLA Ops:
  0.6 2.7 %constant_dynamic-slice_fusion.1 = bf16[640,1280]{1,0:T(8,128)(2,1)} fusion(bf16[2560,1280]{1,0:T(8,128)(2,1)} %refs_0_.1, s32[]{:T(128)S(6)} %select_n.32), kind=kLoop, calls=%fused_computation.10 | loop fusion | bytes 3276804 | tf_op jit(solution)/shard_map/dynamic_slice | solution.py:642
  6.2 3.4 %pack.6 = (bf16[2,2,64,1920]{3,2,1,0:T(8,128)(2,1)S(1)}, bf16[2,2,64,1920]{3,2,1,0:T(8,128)(2,1)}) custom-call(s32[125]{0:T(128)S(1)} %concatenate.10.vector, bf16[2,2,192,2560]{3,2,1,0:T(8,128)(2,1)} %bitcast.44), custom_call_target="tpu_custom_call" | custom-call | flops 1 | bytes 1 | tf_op jit(solution)/shard_map/pack/pallas_call | solution.py:100
  9.6 4.1 %collective-permute-start.7 = (bf16[2,2,64,1920]{3,2,1,0:T(8,128)(2,1)S(1)}, bf16[2,2,64,1920]{3,2,1,0:T(8,128)(2,1)}, u32[]{:S(2)}, u32[]{:S(2)}) collective-permute-start(bf16[2,2,64,1920]{3,2,1,0:T(8,128)(2,1)S(1)} %get-tuple-element.90), channel_id=1, source_target_pairs={{0,8},{8,16},{16,24},{1,9},{9,17},{17,25},{2,10},{10,18},{18,26},{... | collective-permute-start | bytes 2949128 | tf_op jit(solution)/shard_map/ppermute | solution.py:559
  16.6 16.2 %collective-permute-done.7.refs_2_.refs_3_ = bf16[2,2,64,1920]{3,2,1,0:T(8,128)(2,1)} collective-permute-done((bf16[2,2,64,1920]{3,2,1,0:T(8,128)(2,1)S(1)}, bf16[2,2,64,1920]{3,2,1,0:T(8,128)(2,1)}, u32[]{:S(2)}, u32[]{:S(2)}) %collective-permute-start.7) | collective-permute-done | bytes 983072 | tf_op jit(solution)/shard_map/ppermute | solution.py:559
  38.0 3.3 %pack.7 = bf16[2,192,1920]{2,1,0:T(8,128)(2,1)} custom-call(s32[125]{0:T(128)S(1)} %concatenate.10.vector, bf16[2,192,2560]{2,1,0:T(8,128)(2,1)} %bitcast.49), custom_call_target="tpu_custom_call" | custom-call | flops 1 | bytes 1 | tf_op jit(solution)/shard_map/pack/pallas_call | solution.py:100
  43.3 12.6 %collective-permute-done.8.refs_3_.refs_4_ = bf16[2,2,64,1920]{3,2,1,0:T(8,128)(2,1)} collective-permute-done((bf16[2,2,64,1920]{3,2,1,0:T(8,128)(2,1)}, bf16[2,2,64,1920]{3,2,1,0:T(8,128)(2,1)}, u32[]{:S(2)}, u32[]{:S(2)}) %collective-permute-start.8) | collective-permute-done | bytes 983072 | tf_op jit(solution)/shard_map/ppermute | solution.py:559
  58.0 4.3 %collective-permute-start.18 = (bf16[2,192,1920]{2,1,0:T(8,128)(2,1)}, bf16[2,192,1920]{2,1,0:T(8,128)(2,1)}, u32[]{:S(2)}, u32[]{:S(2)}) collective-permute-start(bf16[2,192,1920]{2,1,0:T(8,128)(2,1)} %pack.7), channel_id=1, source_target_pairs={{0,2},{2,4},{4,6},{1,3},{3,5},{5,7},{8,10},{10,12},{12,14},{9,11},... | collective-permute-start | bytes 4423688 | tf_op jit(solution)/shard_map/ppermute | solution.py:559
  66.8 22.7 %attend_own.1.own.own_stat = bf16[2,192,2688]{2,1,0:T(8,128)(2,1)S(1)} custom-call(s32[125]{0:T(128)S(1)} %concatenate.10.vector, bf16[2,192,2560]{2,1,0:T(8,128)(2,1)} %bitcast.51, bf16[2,2,192,2560]{3,2,1,0:T(8,128)(2,1)} %bitcast.47, bf16[2,2,64,1920]{3,2,1,0:T(8,128)(2,1)} %collective-permute-done.7.refs_2_.refs_3_, ...), custom_call_target="tpu_custom_call" | custom-call | flops 20000000000 | bytes 1 | tf_op jit(solution)/shard_map/attend_own/pallas_call | solution.py:255
  90.9 9.7 %collective-permute-done.11.refs_2_ = bf16[640,1280]{1,0:T(8,128)(2,1)} collective-permute-done((bf16[640,1280]{1,0:T(8,128)(2,1)S(1)}, bf16[640,1280]{1,0:T(8,128)(2,1)}, u32[]{:S(2)}, u32[]{:S(2)}) %collective-permute-start.11) | collective-permute-done | bytes 1638432 | tf_op jit(solution)/shard_map/ppermute | solution.py:569
  104.2 7.9 %collective-permute-done.19.refs_1_ = bf16[2,192,1920]{2,1,0:T(8,128)(2,1)} collective-permute-done((bf16[2,192,1920]{2,1,0:T(8,128)(2,1)}, bf16[2,192,1920]{2,1,0:T(8,128)(2,1)}, u32[]{:S(2)}, u32[]{:S(2)}) %collective-permute-start.19) | collective-permute-done | bytes 1474592 | tf_op jit(solution)/shard_map/ppermute | solution.py:559
  113.4 26.2 %attend_visitors.3 = (bf16[2,192,2048]{2,1,0:T(8,128)(2,1)}, bf16[2,192,2048]{2,1,0:T(8,128)(2,1)}) custom-call(s32[125]{0:T(128)S(1)} %concatenate.10.vector, bf16[2,192,1920]{2,1,0:T(8,128)(2,1)} %collective-permute-done.18.refs_0_, bf16[2,192,1920]{2,1,0:T(8,128)(2,1)} %collective-permute-done.19.refs_1_, bf16[2,2,192,2560]{3,2,1,0:T(8,128)(2,1)S(1)} %bitcast.48, ...), custom_call_target="tpu_custom_call" | custom-call | flops 1 | bytes 1 | tf_op jit(solution)/shard_map/attend_visitors/pallas_call | solution.py:255
  139.6 3.2 %collective-permute-start.20 = (bf16[2,192,2048]{2,1,0:T(8,128)(2,1)}, bf16[2,192,2048]{2,1,0:T(8,128)(2,1)}, u32[]{:S(2)}, u32[]{:S(2)}) collective-permute-start(bf16[2,192,2048]{2,1,0:T(8,128)(2,1)} %get-tuple-element.112), channel_id=1, source_target_pairs={{0,2},{2,4},{4,6},{1,3},{3,5},{5,7},{8,10},{10,12},{12,14},{9,11},... | collective-permute-start | bytes 4718600 | tf_op jit(solution)/shard_map/ppermute | solution.py:559
  145.1 3.4 %collective-permute-done.15.refs_3_ = bf16[640,1280]{1,0:T(8,128)(2,1)} collective-permute-done((bf16[640,1280]{1,0:T(8,128)(2,1)S(1)}, bf16[640,1280]{1,0:T(8,128)(2,1)}, u32[]{:S(2)}, u32[]{:S(2)}) %collective-permute-start.15) | collective-permute-done | bytes 1638432 | tf_op jit(solution)/shard_map/ppermute | solution.py:564
  148.5 4.7 %collective-permute-start.17 = (bf16[640,1280]{1,0:T(8,128)(2,1)}, bf16[640,1280]{1,0:T(8,128)(2,1)S(1)}, u32[]{:S(2)}, u32[]{:S(2)}) collective-permute-start(bf16[640,1280]{1,0:T(8,128)(2,1)} %collective-permute-done.15.refs_3_), channel_id=1, source_target_pairs={{0,16},{8,24},{16,0},{24,8},{1,17},{9,25},{17,1},{25,9},{2,18},{10... | collective-permute-start | bytes 4915208 | tf_op jit(solution)/shard_map/ppermute | solution.py:569
  153.5 2.8 %constant_dynamic-slice_fusion = bf16[640,1280]{1,0:T(8,128)(2,1)} fusion(bf16[2560,1280]{1,0:T(8,128)(2,1)} %refs_0_.1, s32[]{:T(128)S(6)} %select_n.36), kind=kLoop, calls=%fused_computation.9 | loop fusion | bytes 3276804 | tf_op jit(solution)/shard_map/dynamic_slice | solution.py:642
  156.4 25.8 %collective-permute-done.20.left = bf16[2,192,2048]{2,1,0:T(8,128)(2,1)} collective-permute-done((bf16[2,192,2048]{2,1,0:T(8,128)(2,1)}, bf16[2,192,2048]{2,1,0:T(8,128)(2,1)}, u32[]{:S(2)}, u32[]{:S(2)}) %collective-permute-start.20) | collective-permute-done | bytes 1572896 | tf_op jit(solution)/shard_map/ppermute | solution.py:559
  182.7 7.9 %combine.1 = bf16[2,192,2560]{2,1,0:T(8,128)(2,1)S(1)} custom-call(s32[125]{0:T(128)S(1)} %concatenate.10.vector, bf16[2,192,2688]{2,1,0:T(8,128)(2,1)S(1)} %copy-done.15, bf16[2,192,2688]{2,1,0:T(8,128)(2,1)S(1)} %copy-done.15, bf16[2,192,2048]{2,1,0:T(8,128)(2,1)} %collective-permute-done.20.left, bf16[2,192,2048]{2,1,0:T(8,128)(2,1)} %collective-permute-done.21.right, ...), custom_call_target="tpu_custom_call" | custom-call | flops 20000000000 | bytes 1 | tf_op jit(solution)/shard_map/combine/pallas_call | solution.py:332
  196.3 4.5 %project.4.own_part = bf16[1,384,1280]{2,1,0:T(8,128)(2,1)S(1)} custom-call(s32[1]{0:T(128)} %bitcast.2.place, bf16[384,2560]{1,0:T(8,128)(2,1)S(1)} %bitcast.39, bf16[2560,1280]{1,0:T(8,128)(2,1)S(1)} %bitcast.43), custom_call_target="tpu_custom_call" | custom-call | flops 1 | bytes 1 | tf_op jit(solution)/shard_map/project/pallas_call | solution.py:402
  208.4 10.2 %project.3.refs_3_ = f32[3,384,1280]{2,1,0:T(8,128)S(1)} custom-call(s32[1]{0:T(128)} %bitcast.2.place, bf16[384,2560]{1,0:T(8,128)(2,1)S(1)} %bitcast.40, bf16[640,1280]{1,0:T(8,128)(2,1)S(1)} %copy-done.5, bf16[640,1280]{1,0:T(8,128)(2,1)S(1)} %copy-done.9, bf16[640,1280]{1,0:T(8,128)(2,1)} %collective-permute-done.11.refs_2_, ...), custom_call_target="tpu_custom_call" | custom-call | flops 1 | bytes 1 | tf_op jit(solution)/shard_map/project/pallas_call | solution.py:402
  218.7 4.4 %pick.1 = (bf16[4,384,1280]{2,1,0:T(8,128)(2,1)S(1)}, f32[4,1,1280]{2,1,0:T(1,128)S(1)}) custom-call(s32[8]{0:T(128)S(1)} %reshape.118.place, bf16[384,2560]{1,0:T(8,128)(2,1)} %bitcast.14.own_hidden, bf16[384,2560]{1,0:T(8,128)(2,1)} %collective-permute-done.22.other_hidden, f32[1,2560]{1,0:T(1,128)S(1)} %get-tuple-element.93.own_gate, ...), custom_call_target="tpu_custom_call" | custom-call | flops 1 | bytes 1 | tf_op jit(solution)/shard_map/pick/pallas_call | solution.py:442
  223.2 4.6 %mix.1 = (bf16[1,384,1280]{2,1,0:T(8,128)(2,1)S(1)}, f32[384,128]{1,0:T(8,128)S(1)}) custom-call(bf16[4,384,1280]{2,1,0:T(8,128)(2,1)S(1)} %get-tuple-element.135.hidden.refs_0_.refs_1_.refs_2_, f32[4,1,1280]{2,1,0:T(1,128)S(1)} %get-tuple-element.133.gate, bf16[1,384,1280]{2,1,0:T(8,128)(2,1)S(1)} %project.4.own_part, ...), custom_call_target="tpu_custom_call" | custom-call | flops 1 | bytes 1 | tf_op jit(solution)/shard_map/mix/pallas_call | solution.py:481
  231.5 6.0 %project.5.refs_3_.refs_4_.refs_5_ = bf16[3,384,1280]{2,1,0:T(8,128)(2,1)S(1)} custom-call(s32[1]{0:T(128)} %bitcast.2.place, bf16[384,2560]{1,0:T(8,128)(2,1)S(1)} %bitcast.41, bf16[640,1280]{1,0:T(8,128)(2,1)} %collective-permute-done.23.refs_0_, bf16[640,1280]{1,0:T(8,128)(2,1)} %collective-permute-done.24.refs_1_, ...), custom_call_target="tpu_custom_call" | custom-call | flops 1 | bytes 1 | tf_op jit(solution)/shard_map/project/pallas_call | solution.py:402
  239.5 5.1 %collective-permute-done.27.refs_6_.refs_7_.refs_8_ = bf16[3,384,1280]{2,1,0:T(8,128)(2,1)} collective-permute-done((bf16[3,384,1280]{2,1,0:T(8,128)(2,1)S(1)}, bf16[3,384,1280]{2,1,0:T(8,128)(2,1)}, u32[]{:S(2)}, u32[]{:S(2)}) %collective-permute-start.27) | collective-permute-done | bytes 2949152 | tf_op jit(solution)/shard_map/ppermute | solution.py:569
  247.9 7.6 %finish.1 = (bf16[384,2560]{1,0:T(8,128)(2,1)}, bf16[384,2560]{1,0:T(8,128)(2,1)}) custom-call(s32[2]{0:T(128)S(1)} %pad_add_fusion.1.place, f32[4,1,1280]{2,1,0:T(1,128)S(1)} %get-tuple-element.133.gate, f32[1,2560]{1,0:T(1,128)S(1)} %get-tuple-element.148.scale, f32[1,2560]{1,0:T(1,128)S(1)} %get-tuple-element.147.shift_by, ...), custom_call_target="tpu_custom_call" | custom-call | flops 1 | bytes 1 | tf_op jit(solution)/shard_map/finish/pallas_call | solution.py:535
  (100 shorter events, 52.5 us)
Async XLA Ops:
  3.4 52.6 %collective-permute-start.6 = (bf16[640,1280]{1,0:T(8,128)(2,1)}, bf16[640,1280]{1,0:T(8,128)(2,1)S(1)}, u32[]{:S(2)}, u32[]{:S(2)}) collective-permute-start(bf16[640,1280]{1,0:T(8,128)(2,1)} %constant_dynamic-slice_fusion.1), channel_id=1, source_target_pairs={{0,2},{2,4},{4,6},{6,0},{1,3},{3,5},{5,7},{7,1},{8,10},{10,12},{12... | collective-permute-start | bytes 4915208 | tf_op jit(solution)/shard_map/ppermute | solution.py:564
  9.6 23.2 %collective-permute-start.7 = (bf16[2,2,64,1920]{3,2,1,0:T(8,128)(2,1)S(1)}, bf16[2,2,64,1920]{3,2,1,0:T(8,128)(2,1)}, u32[]{:S(2)}, u32[]{:S(2)}) collective-permute-start(bf16[2,2,64,1920]{3,2,1,0:T(8,128)(2,1)S(1)} %get-tuple-element.90), channel_id=1, source_target_pairs={{0,8},{8,16},{16,24},{1,9},{9,17},{17,25},{2,10},{10,18},{18,26},{... | collective-permute-start | bytes 2949128 | tf_op jit(solution)/shard_map/ppermute | solution.py:559
  13.7 42.2 %collective-permute-start.8 = (bf16[2,2,64,1920]{3,2,1,0:T(8,128)(2,1)}, bf16[2,2,64,1920]{3,2,1,0:T(8,128)(2,1)}, u32[]{:S(2)}, u32[]{:S(2)}) collective-permute-start(bf16[2,2,64,1920]{3,2,1,0:T(8,128)(2,1)} %get-tuple-element.92), channel_id=1, source_target_pairs={{8,0},{16,8},{24,16},{9,1},{17,9},{25,17},{10,2},{18,10},{26,18},{... | collective-permute-start | bytes 2949128 | tf_op jit(solution)/shard_map/ppermute | solution.py:559
  32.8 2.7 %collective-permute-start.9 = (f32[1,2560]{1,0:T(1,128)S(1)}, f32[1,2560]{1,0:T(1,128)S(1)}, u32[]{:S(2)}, u32[]{:S(2)}) collective-permute-start(f32[1,2560]{1,0:T(1,128)S(1)} %get-tuple-element.93.own_gate), channel_id=1, source_target_pairs={{0,1},{1,0},{2,3},{3,2},{4,5},{5,4},{6,7},{7,6},{8,9},{9,8},{10,11... | collective-permute-start | bytes 30728 | tf_op jit(solution)/shard_map/ppermute | solution.py:569
  43.1 47.8 %collective-permute-start.12 = (bf16[640,1280]{1,0:T(8,128)(2,1)}, bf16[640,1280]{1,0:T(8,128)(2,1)S(1)}, u32[]{:S(2)}, u32[]{:S(2)}) collective-permute-start(bf16[640,1280]{1,0:T(8,128)(2,1)} %constant_dynamic-slice_fusion.1), channel_id=1, source_target_pairs={{0,6},{2,0},{4,2},{6,4},{1,7},{3,1},{5,3},{7,5},{8,14},{10,8},{12,... | collective-permute-start | bytes 4915208 | tf_op jit(solution)/shard_map/ppermute | solution.py:564
  55.9 56.1 %collective-permute-start.19 = (bf16[2,192,1920]{2,1,0:T(8,128)(2,1)}, bf16[2,192,1920]{2,1,0:T(8,128)(2,1)}, u32[]{:S(2)}, u32[]{:S(2)}) collective-permute-start(bf16[2,192,1920]{2,1,0:T(8,128)(2,1)} %pack.7), channel_id=1, source_target_pairs={{2,0},{4,2},{6,4},{3,1},{5,3},{7,5},{10,8},{12,10},{14,12},{11,9},... | collective-permute-start | bytes 4423688 | tf_op jit(solution)/shard_map/ppermute | solution.py:559
  58.0 55.4 %collective-permute-start.18 = (bf16[2,192,1920]{2,1,0:T(8,128)(2,1)}, bf16[2,192,1920]{2,1,0:T(8,128)(2,1)}, u32[]{:S(2)}, u32[]{:S(2)}) collective-permute-start(bf16[2,192,1920]{2,1,0:T(8,128)(2,1)} %pack.7), channel_id=1, source_target_pairs={{0,2},{2,4},{4,6},{1,3},{3,5},{5,7},{8,10},{10,12},{12,14},{9,11},... | collective-permute-start | bytes 4423688 | tf_op jit(solution)/shard_map/ppermute | solution.py:559
  65.6 35.0 %collective-permute-start.11 = (bf16[640,1280]{1,0:T(8,128)(2,1)S(1)}, bf16[640,1280]{1,0:T(8,128)(2,1)}, u32[]{:S(2)}, u32[]{:S(2)}) collective-permute-start(bf16[640,1280]{1,0:T(8,128)(2,1)S(1)} %collective-permute-done.6.refs_0_), channel_id=1, source_target_pairs={{0,16},{8,24},{16,0},{24,8},{1,17},{9,25},{17,1},{25,9},{2,18},{10... | collective-permute-start | bytes 4915208 | tf_op jit(solution)/shard_map/ppermute | solution.py:569
  65.6 35.0 %collective-permute-start.10 = (bf16[640,1280]{1,0:T(8,128)(2,1)S(1)}, bf16[640,1280]{1,0:T(8,128)(2,1)S(1)}, u32[]{:S(2)}, u32[]{:S(2)}) collective-permute-start(bf16[640,1280]{1,0:T(8,128)(2,1)S(1)} %collective-permute-done.6.refs_0_), channel_id=1, source_target_pairs={{0,8},{8,0},{16,24},{24,16},{1,9},{9,1},{17,25},{25,17},{2,10},{10... | collective-permute-start | bytes 4915208 | tf_op jit(solution)/shard_map/ppermute | solution.py:569
  66.8 46.5 %copy-start.16 = (bf16[2,2,24,8,2560]{4,3,2,1,0:T(8,128)(2,1)S(1)}, bf16[2,2,24,8,2560]{4,3,2,1,0:T(8,128)(2,1)}, u32[]{:S(2)}) copy-start(bf16[2,2,24,8,2560]{4,3,2,1,0:T(8,128)(2,1)} %param.13) | copy-start | bytes 11796484
  90.9 48.7 %copy-start.6 = (bf16[640,1280]{1,0:T(8,128)(2,1)}, bf16[640,1280]{1,0:T(8,128)(2,1)S(1)}, u32[]{:S(2)}) copy-start(bf16[640,1280]{1,0:T(8,128)(2,1)S(1)} %collective-permute-done.12.refs_6_) | copy-start | bytes 4915204
  101.8 46.7 %collective-permute-start.15 = (bf16[640,1280]{1,0:T(8,128)(2,1)S(1)}, bf16[640,1280]{1,0:T(8,128)(2,1)}, u32[]{:S(2)}, u32[]{:S(2)}) collective-permute-start(bf16[640,1280]{1,0:T(8,128)(2,1)S(1)} %collective-permute-done.6.refs_0_), channel_id=1, source_target_pairs={{0,2},{2,4},{4,6},{6,0},{1,3},{3,5},{5,7},{7,1},{8,10},{10,12},{12... | collective-permute-start | bytes 4915208 | tf_op jit(solution)/shard_map/ppermute | solution.py:564
  101.8 46.7 %collective-permute-start.14 = (bf16[640,1280]{1,0:T(8,128)(2,1)S(1)}, bf16[640,1280]{1,0:T(8,128)(2,1)}, u32[]{:S(2)}, u32[]{:S(2)}) collective-permute-start(bf16[640,1280]{1,0:T(8,128)(2,1)S(1)} %collective-permute-done.12.refs_6_), channel_id=1, source_target_pairs={{0,16},{8,24},{16,0},{24,8},{1,17},{9,25},{17,1},{25,9},{2,18},{10... | collective-permute-start | bytes 4915208 | tf_op jit(solution)/shard_map/ppermute | solution.py:569
  103.0 45.5 %collective-permute-start.13 = (bf16[640,1280]{1,0:T(8,128)(2,1)S(1)}, bf16[640,1280]{1,0:T(8,128)(2,1)}, u32[]{:S(2)}, u32[]{:S(2)}) collective-permute-start(bf16[640,1280]{1,0:T(8,128)(2,1)S(1)} %collective-permute-done.12.refs_6_), channel_id=1, source_target_pairs={{0,8},{8,0},{16,24},{24,16},{1,9},{9,1},{17,25},{25,17},{2,10},{10... | collective-permute-start | bytes 4915208 | tf_op jit(solution)/shard_map/ppermute | solution.py:569
  139.6 42.6 %collective-permute-start.20 = (bf16[2,192,2048]{2,1,0:T(8,128)(2,1)}, bf16[2,192,2048]{2,1,0:T(8,128)(2,1)}, u32[]{:S(2)}, u32[]{:S(2)}) collective-permute-start(bf16[2,192,2048]{2,1,0:T(8,128)(2,1)} %get-tuple-element.112), channel_id=1, source_target_pairs={{0,2},{2,4},{4,6},{1,3},{3,5},{5,7},{8,10},{10,12},{12,14},{9,11},... | collective-permute-start | bytes 4718600 | tf_op jit(solution)/shard_map/ppermute | solution.py:559
  142.8 39.4 %collective-permute-start.21 = (bf16[2,192,2048]{2,1,0:T(8,128)(2,1)}, bf16[2,192,2048]{2,1,0:T(8,128)(2,1)}, u32[]{:S(2)}, u32[]{:S(2)}) collective-permute-start(bf16[2,192,2048]{2,1,0:T(8,128)(2,1)} %get-tuple-element.113), channel_id=1, source_target_pairs={{2,0},{4,2},{6,4},{3,1},{5,3},{7,5},{10,8},{12,10},{14,12},{11,9},... | collective-permute-start | bytes 4718600 | tf_op jit(solution)/shard_map/ppermute | solution.py:559
  148.5 42.1 %collective-permute-start.17 = (bf16[640,1280]{1,0:T(8,128)(2,1)}, bf16[640,1280]{1,0:T(8,128)(2,1)S(1)}, u32[]{:S(2)}, u32[]{:S(2)}) collective-permute-start(bf16[640,1280]{1,0:T(8,128)(2,1)} %collective-permute-done.15.refs_3_), channel_id=1, source_target_pairs={{0,16},{8,24},{16,0},{24,8},{1,17},{9,25},{17,1},{25,9},{2,18},{10... | collective-permute-start | bytes 4915208 | tf_op jit(solution)/shard_map/ppermute | solution.py:569
  153.2 37.5 %collective-permute-start.16 = (bf16[640,1280]{1,0:T(8,128)(2,1)}, bf16[640,1280]{1,0:T(8,128)(2,1)}, u32[]{:S(2)}, u32[]{:S(2)}) collective-permute-start(bf16[640,1280]{1,0:T(8,128)(2,1)} %collective-permute-done.15.refs_3_), channel_id=1, source_target_pairs={{0,8},{8,0},{16,24},{24,16},{1,9},{9,1},{17,25},{25,17},{2,10},{10... | collective-permute-start | bytes 4915208 | tf_op jit(solution)/shard_map/ppermute | solution.py:569
  182.2 36.5 %collective-permute-start.22 = (bf16[384,2560]{1,0:T(8,128)(2,1)}, bf16[384,2560]{1,0:T(8,128)(2,1)}, u32[]{:S(2)}, u32[]{:S(2)}) collective-permute-start(bf16[384,2560]{1,0:T(8,128)(2,1)} %bitcast.14.own_hidden), channel_id=1, source_target_pairs={{0,1},{1,0},{2,3},{3,2},{4,5},{5,4},{6,7},{7,6},{8,9},{9,8},{10,11... | collective-permute-start | bytes 5898248 | tf_op jit(solution)/shard_map/ppermute | solution.py:569
  190.6 38.1 %collective-permute-start.25 = (bf16[640,1280]{1,0:T(8,128)(2,1)}, bf16[640,1280]{1,0:T(8,128)(2,1)}, u32[]{:S(2)}, u32[]{:S(2)}) collective-permute-start(bf16[640,1280]{1,0:T(8,128)(2,1)} %constant_dynamic-slice_fusion), channel_id=1, source_target_pairs={{0,6},{2,0},{4,2},{6,4},{1,7},{3,1},{5,3},{7,5},{8,14},{10,8},{12,... | collective-permute-start | bytes 4915208 | tf_op jit(solution)/shard_map/ppermute | solution.py:564
  191.3 38.2 %collective-permute-start.23 = (bf16[640,1280]{1,0:T(8,128)(2,1)}, bf16[640,1280]{1,0:T(8,128)(2,1)}, u32[]{:S(2)}, u32[]{:S(2)}) collective-permute-start(bf16[640,1280]{1,0:T(8,128)(2,1)} %collective-permute-done.11.refs_2_), channel_id=1, source_target_pairs={{0,8},{8,0},{16,24},{24,16},{1,9},{9,1},{17,25},{25,17},{2,10},{10... | collective-permute-start | bytes 4915208 | tf_op jit(solution)/shard_map/ppermute | solution.py:569
  193.9 37.5 %collective-permute-start.24 = (bf16[640,1280]{1,0:T(8,128)(2,1)}, bf16[640,1280]{1,0:T(8,128)(2,1)}, u32[]{:S(2)}, u32[]{:S(2)}) collective-permute-start(bf16[640,1280]{1,0:T(8,128)(2,1)} %collective-permute-done.16.refs_4_), channel_id=1, source_target_pairs={{0,16},{8,24},{16,0},{24,8},{1,17},{9,25},{17,1},{25,9},{2,18},{10... | collective-permute-start | bytes 4915208 | tf_op jit(solution)/shard_map/ppermute | solution.py:569
  200.8 22.4 %collective-permute-start.26 = (bf16[1,384,1280]{2,1,0:T(8,128)(2,1)S(1)}, bf16[1,384,1280]{2,1,0:T(8,128)(2,1)}, u32[]{:S(2)}, u32[]{:S(2)}) collective-permute-start(bf16[1,384,1280]{2,1,0:T(8,128)(2,1)S(1)} %project.4.own_part), channel_id=1, source_target_pairs={{0,1},{1,0},{2,3},{3,2},{4,5},{5,4},{6,7},{7,6},{8,9},{9,8},{10,11... | collective-permute-start | bytes 2949128 | tf_op jit(solution)/shard_map/ppermute | solution.py:569
  237.5 7.1 %collective-permute-start.27 = (bf16[3,384,1280]{2,1,0:T(8,128)(2,1)S(1)}, bf16[3,384,1280]{2,1,0:T(8,128)(2,1)}, u32[]{:S(2)}, u32[]{:S(2)}) collective-permute-start(bf16[3,384,1280]{2,1,0:T(8,128)(2,1)S(1)} %project.5.refs_3_.refs_4_.refs_5_), channel_id=1, source_target_pairs={{0,1},{1,0},{2,3},{3,2},{4,5},{5,4},{6,7},{7,6},{8,9},{9,8},{10,11... | collective-permute-start | bytes 8847368 | tf_op jit(solution)/shard_map/ppermute | solution.py:569
  (18 other events, 214.5 us)
